TPU v7x, 256 devices: a whole 4x4x8 slice. The times are simulated.
256 devices in a mesh: ta: 16 (over z, core), wa: 16 (over y, x).
Axes of the slice: x: 4, y: 4, z: 8, core: 2. Of those that a mesh axis runs over, the one named last changes fastest.
Arguments:
- amplitudes: float32 [96, 512, 512], P('wa', 'ta'), may hold values from -6 to 6
- integrals: float32 [96, 512, 32, 512], P('wa', None, 'ta'), may hold values from -0.02734375 to 0.02734375
- blockmap: int32 [96, 32, 8, 8], P('wa', 'ta'), may hold values 0 or 1
- irrep_occ: int32 [96], replicated, may hold values from 0 to 1, as said below
- irrep_virt: int32 [512], replicated, may hold values from 0 to 1, as said below
Outputs:
- cycle_term: float32 [512, 32, 512], P('wa', 'ta')
Inputs may be any that keep to these rules, and one draw needn't show every extreme that they name: `irrep_occ`: labels are constant over each aligned group of 8 occupied orbitals. `irrep_virt`: labels are constant over each aligned block of 64 virtual orbitals.
All inputs are finite; a program needn't handle non-finite values. No bound on the sum of `blockmap` on one device may be relied on, other than what follows from the above.
Results may differ from a plain program's by a relative error of at most 0.00007.
Values sent between devices are 32-bit elements; how exact they have to be, the bound alone decides.
A program may use at most 128 MiB of HBM per device.

v0:
```python
import jax
import jax.numpy as jnp
from jax import lax
from jax.sharding import PartitionSpec as P

BLK = 64


def screen(values, occ_labels, row_labels, col_labels):
    parity = (occ_labels[:, None, None] + row_labels[None, :, None] + col_labels[None, None, :]) % 2
    return jnp.where(parity == 0, values, jnp.float32(0.0))


def local(amplitudes, integrals, blockmap, irrep_occ, irrep_virt):
    local_occ = amplitudes.shape[0]
    local_rows = amplitudes.shape[1]
    virtuals = amplitudes.shape[2]
    local_cols = integrals.shape[2]
    occ_labels = lax.dynamic_slice_in_dim(irrep_occ, lax.axis_index("wa") * local_occ, local_occ)
    blocks = blockmap.astype(jnp.float32)
    spread = jnp.repeat(jnp.repeat(blocks, BLK, axis=2), BLK, axis=3)
    masked = integrals * jnp.transpose(spread, (0, 2, 1, 3))
    flat_weights = masked.reshape(local_occ, virtuals, local_cols * virtuals)
    row_labels = lax.dynamic_slice_in_dim(irrep_virt, lax.axis_index("ta") * local_rows, local_rows)
    screened = screen(amplitudes, occ_labels, row_labels, irrep_virt)
    received = lax.all_to_all(screened, "ta", split_axis=2, concat_axis=1, tiled=True)
    combined = 2.0 * screened - jnp.transpose(received, (0, 2, 1))
    partial_sum = jnp.einsum(
        "kac,kcn->an",
        lax.all_gather(combined, "ta", axis=1, tiled=True),
        flat_weights,
        precision=lax.Precision.HIGHEST,
    )
    shared = lax.psum_scatter(partial_sum, "wa", scatter_dimension=0, tiled=True)
    return shared.reshape(shared.shape[0], local_cols, virtuals)


def solution(mesh):
    in_specs = (P("wa", "ta", None), P("wa", None, "ta", None), P("wa", "ta", None, None), P(), P())
    out_specs = P("wa", "ta", None)
    return jax.shard_map(local, mesh=mesh, in_specs=in_specs, out_specs=out_specs, check_vma=False)
```

profile of v0, /device:TPU:2, one launch (start us, length us, event | category | flops | bytes accessed | tf_op | source)
XLA Modules:
  0.0 196.5 jit_solution(156881647135675725)
XLA Ops:
  6.5 0.8 dynamic_slice.7
  7.4 0.7 dynamic_slice.6
  8.1 0.1 broadcast_add_fusion
  8.2 1.2 fusion.2
  9.4 0.8 copy.12
  10.2 0.8 reshape.50
  11.0 22.1 %all_to_all.18 = f32[16,1,6144]{2,1,0:T(1,128)S(1)} all-to-all(f32[16,1,6144]{2,1,0:T(1,128)S(1)} %reshape.50), channel_id=1, replica_groups=mesh['ta'=16,'wa'=16] {'ta'}, dimensions={0} | all-to-all | bytes 786432 | tf_op jit(solution)/shard_map/all_to_all | solution.py:26
  33.1 0.5 broadcast.34
  33.6 1.6 reduce
  35.1 0.7 reshape.51
  35.9 2.1 %copy.19 = f32[6,32,16,32]{1,2,3,0:T(8,128)} copy(f32[6,32,16,32]{1,0,3,2:T(8,128)S(1)} %bitcast.26) | data formatting | bytes 786432 | tf_op jit(solution)/shard_map/all_to_all | solution.py:26
  37.9 2.0 %all_to_all.16 = f32[6,512,32]{1,2,0:T(8,128)S(1)} reshape(f32[6,16,32,32]{2,1,3,0:T(8,128)} %bitcast.28) | data formatting | bytes 786432 | tf_op jit(solution)/shard_map/all_to_all | solution.py:26
  40.0 1.0 bitcast_subtract_fusion
  41.0 0.0 all-gather.2.cloned.1.call-update
  41.0 0.2 reduce-scatter.2.cloned.1.call-start
  41.3 0.1 copy.14
  41.4 0.2 broadcast_in_dim.14
  41.5 0.1 reshape.45
  41.7 19.2 %copy.15 = f32[6,512,2,512]{1,3,2,0:T(8,128)} copy(f32[6,512,2,512]{3,2,1,0:T(2,128)} %param.6) | data formatting | bytes 25165824 | tf_op args[1]
  60.9 11.2 %bitcast_multiply_fusion = f32[6,512,2,512]{1,3,2,0:T(8,128)} fusion(f32[6,512,2,512]{1,3,2,0:T(8,128)} %copy.15, f32[6,2,512,8]{2,3,1,0:T(8,128)S(1)} %reshape.45), kind=kLoop, calls=%fused_computation | loop fusion | flops 3145728 | bytes 25362432 | tf_op jit(solution)/shard_map/mul | solution.py:22
  72.0 13.3 %all-gather.2.cloned.1.call-done = f32[6,512,512]{2,1,0:T(8,128)} async-done(((f32[6,32,512]{2,1,0:T(8,128)}), f32[6,512,512]{2,1,0:T(8,128)}) %all-gather.2.cloned.1.call-update) | async-done | bytes 6291472 | tf_op jit(solution)/shard_map/all_gather | solution.py:30
  85.3 24.9 %convolution_bitcast_fusion = f32[512,1024]{1,0:T(8,128)} fusion(f32[6,512,512]{2,1,0:T(8,128)} %all-gather.2.cloned.1.call-done, f32[6,512,1024]{1,2,0:T(8,128)} %bitcast.25), kind=kOutput, calls=%fused_computation.1 | convolution fusion | flops 19327352832 | bytes 20971520 | tf_op jit(solution)/shard_map/kac,kcn->an/dot_general | solution.py:28
  110.3 77.8 %reduce-scatter.2.cloned.1.call-done = f32[32,1024]{1,0:T(8,128)} async-done(((f32[512,1024]{1,0:T(8,128)}), f32[32,1024]{1,0:T(8,128)}) %reduce-scatter.2.cloned.1.call-update) | async-done | bytes 131088 | tf_op jit(solution)/shard_map/reduce_scatter | solution.py:34
  188.0 1.7 reshape.48
  (9 shorter events, 0.0 us)
Async XLA Ops:
  6.5 33.4 %copy-start.2 = (s32[512]{0:T(512)S(1)}, s32[512]{0:T(512)}, u32[]{:S(2)}) copy-start(s32[512]{0:T(512)} %param.9) | copy-start | bytes 6148
  6.5 33.4 %copy-start = (f32[6,32,512]{2,1,0:T(8,128)S(1)}, f32[6,32,512]{2,1,0:T(8,128)}, u32[]{:S(2)}) copy-start(f32[6,32,512]{2,1,0:T(8,128)} %param.5) | copy-start | bytes 1179652
  6.5 34.7 %copy-start.1 = (s32[6,2,8,8]{3,2,1,0:T(8,128)S(1)}, s32[6,2,8,8]{3,2,1,0:T(8,128)}, u32[]{:S(2)}) copy-start(s32[6,2,8,8]{3,2,1,0:T(8,128)} %param.7) | copy-start | bytes 9220
  6.5 78.8 %all-gather.2.cloned.1.call-start = ((), (), s32[]{:S(2)}) async-start(), calls=%async_computation.2 | async-start | bytes 6684672 | tf_op jit(solution)/shard_map/all_gather | solution.py:30
  41.0 147.0 %reduce-scatter.2.cloned.1.call-start = ((), (), s32[]{:S(2)}) async-start(), calls=%async_computation.3 | async-start | bytes 2228224 | tf_op jit(solution)/shard_map/reduce_scatter | solution.py:34
Sparse Core Ops, SparseCore 0:
  41.2 44.1 all-gather.1
  110.4 77.6 reduce-scatter.1
where the time goes:
time: 197 us
  waiting for transfers between devices  91.1 us (46%)
  local copies, waits for them, and re-layouts  29.7 us (15%)
  matrix products  24.9 us (13%)
  blocking collectives  22.1 us (11%)
  other arithmetic  15.1 us (8%)
  between operations  13.5 us (7%)
    reduce_scatter x1, waiting for transfers between devices, local(): lax.psum_scatter(partial_sum, 'wa', scatter_dimension=0, tiled=True)  77.8 us
    dot_general x1, matrix products, local(): jnp.einsum('kac,kcn->an', lax.all_gather(combined, 'ta', axis=1, tiled=Tr...  24.9 us
    all_to_all x1, blocking collectives, local(): lax.all_to_all(screened, 'ta', split_axis=2, concat_axis=1, tiled=True)  22.1 us
    unnamed x9, local copies, waits for them, and re-layouts  20.7 us
    all_gather x1, waiting for transfers between devices, local(): lax.all_gather(combined, 'ta', axis=1, tiled=True)  13.3 us
    mul x1, other arithmetic, local(): masked = integrals * jnp.transpose(spread, (0, 2, 1, 3))  11.2 us
    all_to_all x3, local copies, waits for them, and re-layouts, local(): lax.all_to_all(screened, 'ta', split_axis=2, concat_axis=1, tiled=True)  4.63 us
  transfers between devices with their start and end apart: 2, of which 2 were waited for; matrix products, arithmetic and copies ran while one was open for 16% of the time, Pallas kernels for 0%

commit v1 on v0

v1 whole, which is shorter than its diff:
```python
import functools

import jax
import jax.numpy as jnp
from jax import lax
from jax.experimental import pallas as pl
from jax.experimental.pallas import tpu as pltpu
from jax.sharding import PartitionSpec as P

MESH = pl.DeviceIdType.MESH
LAG = 2
OCC_L = 6
UNITS = 2 * OCC_L
CHIPS = 8
F32 = jnp.float32
BF16 = jnp.bfloat16
TICKS = UNITS + 4 * LAG
DELAY = 1 + 4 * LAG


def split(v):
    hi = v.astype(BF16)
    lo = (v - hi.astype(F32)).astype(BF16)
    return hi, lo


def kernel(amp, w, bm, lv, lo_ref, out, X, Wf, Wh, Wl, bmx, Ch, Cl, acc, RA, RB, RD, S, QA, QB, QD,
           w_sem, x_sem, right_recv, left_recv, sib_recv, ring_send, rs_send, rs_recv):
    t = lax.axis_index("ta")
    wi = lax.axis_index("wa")
    z, h = t // 2, t % 2
    y, x = wi // 4, wi % 4

    def chip(delta):
        return lax.rem(z + delta + CHIPS, CHIPS)

    z_right = {"ta": chip(1) * 2 + h}
    z_left = {"ta": chip(-1) * 2 + h}
    sibling = {"ta": z * 2 + (1 - h)}

    def step(i, delta):
        return lax.rem(i + delta + 4, 4)

    x_next, x_prev = {"wa": y * 4 + step(x, 1)}, {"wa": y * 4 + step(x, -1)}
    y_next, y_prev = {"wa": step(y, 1) * 4 + x}, {"wa": step(y, -1) * 4 + x}

    def rows(zz, hh):
        return pl.ds(pl.multiple_of(zz * 64 + hh * 32, 32), 32)

    own = [
        pltpu.make_async_copy(amp.at[:, :, pl.ds(256 * g, 256)], X.at[:, g, rows(z, h), :], x_sem.at[g])
        for g in range(2)
    ]
    for c in own:
        c.start()

    def w_copy(k):
        return pltpu.make_async_copy(w.at[k], Wf.at[k], w_sem.at[k])

    for k in range(OCC_L):
        w_copy(k).start()

    barrier = pltpu.get_barrier_semaphore()
    neighbours = (z_right, z_left, sibling, x_next, x_prev, y_next, y_prev)
    for d in neighbours:
        pl.semaphore_signal(barrier, inc=1, device_id=d, device_id_type=MESH)

    lane = lax.broadcasted_iota(jnp.int32, (8, 512), 1) // 64
    row = lax.broadcasted_iota(jnp.int32, (8, 512), 0)
    spread = jnp.where(lane == row, 1.0, 0.0).astype(BF16)
    blocks = bm[...].astype(F32).reshape(96, 8).astype(BF16)
    bmx[...] = jnp.dot(blocks, spread, preferred_element_type=F32).reshape(12, 8, 512)
    acc[...] = jnp.zeros_like(acc)

    for c in own:
        c.wait()
    pl.semaphore_wait(barrier, len(neighbours))

    def unit_copy(u, zz, recv_sem, dest, direction):
        ref = X.at[u // 2, u % 2, rows(zz, h), :]
        return pltpu.make_async_remote_copy(
            src_ref=ref, dst_ref=ref, send_sem=ring_send.at[direction], recv_sem=recv_sem,
            device_id=dest, device_id_type=MESH)

    def to_right(u, zz, d):
        return unit_copy(u, zz, right_recv.at[u * 5 + d], z_right, 0)

    def to_left(u, zz, d):
        return unit_copy(u, zz, left_recv.at[u * 5 + d], z_left, 1)

    def to_sibling(u, zz):
        return unit_copy(u, zz, sib_recv.at[u // 2], sibling, 2)

    def w_prep(k):
        for r in range(8):
            bt, j = r // 2, r % 2
            for cb in range(8):
                slab = Wf[k, pl.ds(cb * 512 + r, 64, stride=8), :]
                m = bmx[k * 2 + j, pl.ds(cb, 1), pl.ds(bt * 128, 128)]
                hi, lo = split(slab * m)
                Wh[k, pl.ds(cb * 64, 64), pl.ds(r * 128, 128)] = hi
                Wl[k, pl.ds(cb * 64, 64), pl.ds(r * 128, 128)] = lo

    def compute(k, mh):
        lk = lo_ref[wi * OCC_L + k]
        blk = lax.broadcasted_iota(jnp.int32, (1, 256), 1) // 64
        for g in range(2):
            labels = jnp.zeros((1, 256), jnp.int32)
            for i in range(4):
                labels = jnp.where(blk == i, lv[(4 * g + i) * 64], labels)
            bt = X[k, mh, pl.ds(256 * g, 256), :].T
            for i in range(4):
                a = X[k, g, pl.ds(pl.multiple_of(256 * mh + 64 * i, 64), 64), :]
                lz = lv[(4 * mh + i) * 64]
                mask = ((labels + (lz + lk)) & 1) == 0
                c = jnp.where(mask, 2.0 * a - bt[64 * i:64 * i + 64, :], 0.0)
                hi, lo = split(c)
                Ch[pl.ds(64 * i, 64), pl.ds(256 * g, 256)] = hi
                Cl[pl.ds(64 * i, 64), pl.ds(256 * g, 256)] = lo
        for nb in range(4):
            n = pl.ds(256 * nb, 256)
            wh = Wh[k, :, n]
            p = jnp.dot(Ch[...], wh, preferred_element_type=F32)
            p = p + jnp.dot(Cl[...], wh, preferred_element_type=F32)
            p = p + jnp.dot(Ch[...], Wl[k, :, n], preferred_element_type=F32)
            acc[pl.ds(2 * mh, 2), :, :, n] += p.reshape(2, 4, 32, 256)

    def tick(s, _):
        @pl.when(s < UNITS)
        def _():
            to_right(s, z, 1).start()
            to_left(s, z, 1).start()
            to_sibling(s, z).start()

        for d in range(1, 5):
            u = s - LAG * d
            inside = (u >= 0) & (u < UNITS)
            even = u % 2 == 0

            @pl.when(inside if d < 4 else inside & even)
            def _():
                zz = chip(-d)
                to_right(u, zz, d).wait_recv()
                if d < 3:
                    to_right(u, zz, d + 1).start()
                elif d == 3:
                    @pl.when(even)
                    def _():
                        to_right(u, zz, d + 1).start()
                to_sibling(u, zz).start()

            @pl.when(inside if d < 4 else inside & jnp.logical_not(even))
            def _():
                zz = chip(d)
                to_left(u, zz, d).wait_recv()
                if d < 3:
                    to_left(u, zz, d + 1).start()
                elif d == 3:
                    @pl.when(jnp.logical_not(even))
                    def _():
                        to_left(u, zz, d + 1).start()
                to_sibling(u, zz).start()

        @pl.when((s >= 1) & (s < 1 + OCC_L))
        def _():
            k = s - 1
            w_copy(k).wait()
            w_prep(k)

        v = s - DELAY

        @pl.when((v >= 0) & (v < UNITS))
        def _():
            k, mh = v // 2, v % 2

            @pl.when(mh == 0)
            def _():
                ref = X.at[k, 0]
                pltpu.make_async_copy(ref, ref, sib_recv.at[k]).wait()

            compute(k, mh)

        return 0

    lax.fori_loop(0, UNITS + DELAY, tick, 0)

    def ring_sum(me, nxt, prv, view, bufs, base, result):
        a, b, d = bufs

        def copy(src, dst, i, dest):
            return pltpu.make_async_remote_copy(
                src_ref=src, dst_ref=dst, send_sem=rs_send.at[base + i], recv_sem=rs_recv.at[base + i],
                device_id=dest, device_id_type=MESH)

        first = [
            copy(view(step(me, 2), 0), a.at[0], 0, nxt),
            copy(view(step(me, 2), 1), a.at[1], 1, prv),
            copy(view(step(me, 1), 1), b.at[1], 2, nxt),
            copy(view(step(me, -1), 0), b.at[0], 3, prv),
        ]
        second = [
            copy(view(step(me, 1), 0), d.at[0], 4, nxt),
            copy(view(step(me, -1), 1), d.at[1], 5, prv),
        ]

        def start():
            for c in first:
                c.start()

        def middle():
            for i in range(2):
                first[i].wait_recv()
                ref = view(step(me, 1 if i == 0 else -1), i)
                ref[...] = ref[...] + a[i]
                second[i].start()

        def finish():
            first[2].wait_recv()
            first[3].wait_recv()
            for i in range(2):
                second[i].wait_recv()
                result(i, view(me, i)[...] + b[i] + d[i])

        def drain():
            for c in first + second:
                c.wait_send()

        return start, middle, finish, drain

    def cols(half, i):
        return pl.ds(512 * half + 256 * i, 256)

    def keep(half):
        def result(i, value):
            S[half, i] = value
        return result

    def emit(half):
        def result(i, value):
            for q in range(2):
                out[:, 4 * half + 2 * i + q, :] = value[:, 128 * q:128 * q + 128]
        return result

    def bufs(refs, half):
        return [r.at[half] for r in refs]

    one = [
        ring_sum(x, x_next, x_prev, lambda i, s: acc.at[:, i, :, cols(0, s)], bufs((RA, RB, RD), 0), 0, keep(0)),
        ring_sum(y, y_next, y_prev, lambda i, s: acc.at[i, :, :, cols(1, s)], bufs((RA, RB, RD), 1), 6, keep(1)),
    ]
    two = [
        ring_sum(y, y_next, y_prev, lambda i, s: S.at[0, s, i], bufs((QA, QB, QD), 0), 12, emit(0)),
        ring_sum(x, x_next, x_prev, lambda i, s: S.at[1, s, i], bufs((QA, QB, QD), 1), 18, emit(1)),
    ]
    for p in one:
        p[0]()
    for p in one:
        p[1]()
    for p, q in zip(one, two):
        p[2]()
        q[0]()
    for q in two:
        q[1]()
    for q in two:
        q[2]()
    for p in one + two:
        p[3]()
    for i, ref in enumerate((X.at[:, 0, pl.ds(0, 224), :], X.at[:, 0, pl.ds(0, 224), :], X.at[:, :, pl.ds(0, 256), :])):
        pltpu.make_async_copy(ref, ref, ring_send.at[i]).wait()


def local(amplitudes, integrals, blockmap, irrep_occ, irrep_virt):
    w = integrals.reshape(6, 512, 2, 4, 128).transpose(0, 1, 3, 2, 4).reshape(6, 4096, 128)
    hbm = pl.BlockSpec(memory_space=pl.ANY)
    vmem = pl.BlockSpec(memory_space=pltpu.VMEM)
    smem = pl.BlockSpec(memory_space=pltpu.SMEM)
    DMA = pltpu.SemaphoreType.DMA
    out = pl.pallas_call(
        kernel,
        out_shape=jax.ShapeDtypeStruct((32, 8, 128), F32),
        in_specs=[hbm, hbm, vmem, smem, smem],
        out_specs=vmem,
        scratch_shapes=[
            pltpu.VMEM((6, 2, 512, 256), F32),
            pltpu.VMEM((6, 4096, 128), F32),
            pltpu.VMEM((6, 512, 1024), BF16),
            pltpu.VMEM((6, 512, 1024), BF16),
            pltpu.VMEM((12, 8, 512), F32),
            pltpu.VMEM((256, 512), BF16),
            pltpu.VMEM((256, 512), BF16),
            pltpu.VMEM((4, 4, 32, 1024), F32),
            pltpu.VMEM((2, 2, 4, 32, 256), F32),
            pltpu.VMEM((2, 2, 4, 32, 256), F32),
            pltpu.VMEM((2, 2, 4, 32, 256), F32),
            pltpu.VMEM((2, 2, 4, 32, 256), F32),
            pltpu.VMEM((2, 2, 32, 256), F32),
            pltpu.VMEM((2, 2, 32, 256), F32),
            pltpu.VMEM((2, 2, 32, 256), F32),
            DMA((6,)),
            DMA((2,)),
            DMA((UNITS * 5,)),
            DMA((UNITS * 5,)),
            DMA((6,)),
            DMA((3,)),
            DMA((24,)),
            DMA((24,)),
        ],
        cost_estimate=pl.CostEstimate(flops=10 ** 10, bytes_accessed=14 * 10 ** 6, transcendentals=0),
        compiler_params=pltpu.CompilerParams(
            collective_id=0, has_side_effects=True, vmem_limit_bytes=60 * 1024 * 1024),
    )(amplitudes, w, blockmap, irrep_virt, irrep_occ)
    return out.reshape(32, 4, 2, 128).transpose(0, 2, 1, 3).reshape(32, 2, 512)


def solution(mesh):
    in_specs = (P("wa", "ta", None), P("wa", None, "ta", None), P("wa", "ta", None, None), P(), P())
    out_specs = P("wa", "ta", None)
    return jax.shard_map(local, mesh=mesh, in_specs=in_specs, out_specs=out_specs, check_vma=False)
```

time: 197 us -> 71.9 us (0.36)
  waiting for transfers between devices: 91.1 us -> 0 us
  Pallas kernels: 0 us -> 70.2 us
  local copies, waits for them, and re-layouts: 29.7 us -> 1.57 us
  matrix products: 24.9 us -> 0 us
  blocking collectives: 22.1 us -> 0 us
  other arithmetic: 15.1 us -> 0 us
  between operations: 13.5 us -> 0.01 us
    reduce_scatter x1 -> x0, waiting for transfers between devices: 77.8 us -> none  [local(): lax.psum_scatter(partial_sum, 'wa', scatter_dimension=0, tiled=True)]
    pallas_call x0 -> x1, Pallas kernels: none -> 70.2 us  [local(): pl.pallas_call(kernel, out_shape=jax.ShapeDtypeStruct((32, 8, 128), F32),...]
    dot_general x1 -> x0, matrix products: 24.9 us -> none  [local(): jnp.einsum('kac,kcn->an', lax.all_gather(combined, 'ta', axis=1, tiled=Tr...]
    all_to_all x1 -> x0, blocking collectives: 22.1 us -> none  [local(): lax.all_to_all(screened, 'ta', split_axis=2, concat_axis=1, tiled=True)]
    unnamed x9 -> x1, local copies, waits for them, and re-layouts: 20.7 us -> 1.57 us
    all_gather x1 -> x0, waiting for transfers between devices: 13.3 us -> none  [local(): lax.all_gather(combined, 'ta', axis=1, tiled=True)]
    mul x1 -> x0, other arithmetic: 11.2 us -> none  [local(): masked = integrals * jnp.transpose(spread, (0, 2, 1, 3))]
    all_to_all x3 -> x0, local copies, waits for them, and re-layouts: 4.63 us -> none  [local(): lax.all_to_all(screened, 'ta', split_axis=2, concat_axis=1, tiled=True)]
  transfers between devices with their start and end apart: 2 -> 0, of which waited for: 2 -> 0; matrix products, arithmetic and copies ran while one was open for 16% -> 0% of each run, Pallas kernels for 0% -> 0%
where the time goes in v1:
time: 71.9 us; the launch traced here: 71.7 us
  Pallas kernels  70.2 us (98%)
  local copies, waits for them, and re-layouts  1.57 us (2%)
    pallas_call x1, Pallas kernels, local(): pl.pallas_call(kernel, out_shape=jax.ShapeDtypeStruct((32, 8, 128), F32),...  70.2 us
    unnamed x1, local copies, waits for them, and re-layouts  1.57 us

profile of v1, /device:TPU:2, one launch (start us, length us, event | category | flops | bytes accessed | tf_op | source)
XLA Modules:
  0.0 71.7 jit_solution(12987974501226299871)
XLA Ops:
  0.0 70.2 %shard_map.55 = f32[32,8,128]{2,1,0:T(8,128)} custom-call(f32[6,32,512]{2,1,0:T(8,128)} %amp.1, f32[6,4096,128]{2,1,0:T(8,128)} %bitcast.11, s32[6,2,8,8]{3,2,1,0:T(8,128)} %bm.1, s32[512]{0:T(512)} %lv.1, s32[96]{0:T(128)} %lo_ref.1), custom_call_target="tpu_custom_call" | custom-call | flops 10000000000 | bytes 14000000 | tf_op jit(solution)/shard_map/pallas_call | solution.py:278
  70.2 1.6 %copy.9 = f32[32,2,512]{2,1,0:T(2,128)} copy(f32[32,2,512]{2,1,0:T(2,128)} %bitcast.10) | data formatting | bytes 262144
